TPU v7x, 32 devices: a whole 2x2x4 slice. The times are simulated.
32 devices in a mesh: jobs: 2 (over y), fsdp: 8 (over z, x), grp: 2 (over core).
Axes of the slice: x: 2, y: 2, z: 4, core: 2. Of those that a mesh axis runs over, the one named last changes fastest.
Arguments:
- tokens: bfloat16 [1024, 8192], P(('jobs', 'grp'), 'fsdp'), parts along dimension 0, may hold values from -6 to 6
- cotangent: bfloat16 [1024, 8192], P(('jobs', 'grp'), 'fsdp'), parts along dimension 0, may hold values from -6 to 6
- w_gate: bfloat16 [8192, 16384], P('grp', 'fsdp'), may hold values from -0.0625 to 0.0625
- w_up: bfloat16 [8192, 16384], P('grp', 'fsdp'), may hold values from -0.0625 to 0.0625
- w_down: bfloat16 [16384, 8192], P('fsdp', 'grp'), may hold values from -0.046875 to 0.046875
- adapt_model: bfloat16 [6, 16, 8192], P('jobs', None, 'fsdp'), parts along dimension 0, may hold values from -0.0625 to 0.0625
- adapt_hidden: bfloat16 [6, 16, 16384], P('jobs', None, 'fsdp'), parts along dimension 0, may hold values from -0.19921875 to 0.19921875
- direction_model: float32 [6, 16, 8192], P('jobs', None, 'fsdp'), parts along dimension 0, may hold values from -60 to 60
- direction_hidden: float32 [6, 16, 16384], P('jobs', None, 'fsdp'), parts along dimension 0, may hold values from -60 to 60
- previous_model: float32 [6, 16, 8192], P('jobs', None, 'fsdp'), parts along dimension 0, may hold values from -6 to 6
- previous_hidden: float32 [6, 16, 16384], P('jobs', None, 'fsdp'), parts along dimension 0, may hold values from -6 to 6
- beta_prev: float32 [2], P('jobs'), parts along dimension 0, may hold values from 1000 to 10000
Outputs:
- next_model: float32 [6, 16, 8192], P('jobs', None, 'fsdp'), parts along dimension 0
- next_hidden: float32 [6, 16, 16384], P('jobs', None, 'fsdp'), parts along dimension 0
- alpha_out: float32 [2], P('jobs'), parts along dimension 0
There are 2 independent parts, one for each index of `jobs`. A program takes and returns all parts, laid end to end along the dimension named above; an argument that names none is the same for every part. Nothing has to cross between parts.
All inputs are finite; a program needn't handle non-finite values.
Results may differ from a plain program's by a relative error of at most 0.0029.
Values may be sent and summed in bfloat16 or wider, within the bound.
A program may use at most 320 MiB of HBM per device.

v0:
```python
import jax
import jax.numpy as jnp
from jax import lax
from jax.sharding import PartitionSpec as P

D = 8192
FF = 16384
R = 16


adapter_scale = 2.0


def gated_product(left, right):
    return jnp.dot(left, right, precision=lax.Precision.HIGHEST, preferred_element_type=jnp.float32)


def lowrank_terms(adapt_part, dir_part, tok_part, cot_part):
    left_tok = jnp.concatenate([adapt_part[:2], dir_part[:2]], 0)
    left_cot = jnp.stack([adapt_part[2], dir_part[2]])
    low_tok = jnp.einsum("krn,tn->krt", left_tok, tok_part, preferred_element_type=jnp.float32)
    low_cot = jnp.einsum("krn,tn->krt", left_cot, cot_part, preferred_element_type=jnp.float32)
    return (low_tok, low_cot)


def body(
    tokens,
    cotangent,
    w_gate,
    w_up,
    w_down,
    adapt_model,
    adapt_hidden,
    direction_model,
    direction_hidden,
    previous_model,
    previous_hidden,
    beta_prev,
):
    dir_model = direction_model.astype(jnp.bfloat16)
    dir_hidden = direction_hidden.astype(jnp.bfloat16)
    full_gate, full_up = (
        lax.all_gather(w_gate, "grp", axis=0, tiled=True),
        lax.all_gather(w_up, "grp", axis=0, tiled=True),
    )
    full_down = lax.all_gather(w_down, "grp", axis=1, tiled=True)
    wide_adapt, wide_dir = (
        lax.all_gather(adapt_model, "fsdp", axis=2, tiled=True),
        lax.all_gather(dir_model, "fsdp", axis=2, tiled=True),
    )
    tok_full, cot_full = (
        lax.all_gather(tokens, "fsdp", axis=1, tiled=True),
        lax.all_gather(cotangent, "fsdp", axis=1, tiled=True),
    )
    gate_baseline = jnp.dot(tok_full, full_gate, preferred_element_type=jnp.float32)
    up_baseline = jnp.dot(tok_full, full_up, preferred_element_type=jnp.float32)
    backward_baseline = lax.dot_general(
        cot_full, full_down, (((1,), (1,)), ((), ())), preferred_element_type=jnp.float32
    )
    low_tok, low_cot = lowrank_terms(wide_adapt, wide_dir, tok_full, cot_full)
    projected_gate, projected_up, tangent_projected_gate, tangent_projected_up = (
        low_tok[0],
        low_tok[1],
        low_tok[2],
        low_tok[3],
    )
    projected_cotangent, tangent_projected_cotangent = (low_cot[0], low_cot[1])
    reduced_hidden = adapt_hidden.astype(jnp.float32)
    tan_hidden_dir = dir_hidden.astype(jnp.float32)
    adapter_gate_factor, adapter_up_factor, adapter_down_factor = (
        reduced_hidden[0],
        reduced_hidden[1],
        reduced_hidden[2],
    )
    direction_gate_adapter, direction_up_adapter, direction_down_adapter = (
        tan_hidden_dir[0],
        tan_hidden_dir[1],
        tan_hidden_dir[2],
    )
    gate_preactivation = gate_baseline + adapter_scale * gated_product(
        projected_gate.T, adapter_gate_factor
    )
    up_preactivation = up_baseline + adapter_scale * gated_product(
        projected_up.T, adapter_up_factor
    )
    tangent_gate = adapter_scale * (
        gated_product(tangent_projected_gate.T, adapter_gate_factor)
        + gated_product(projected_gate.T, direction_gate_adapter)
    )
    tangent_up = adapter_scale * (
        gated_product(tangent_projected_up.T, adapter_up_factor)
        + gated_product(projected_up.T, direction_up_adapter)
    )
    sig_gate = jax.nn.sigmoid(gate_preactivation)
    act_gate = gate_preactivation * sig_gate
    slope_one = sig_gate * (1.0 + gate_preactivation * (1.0 - sig_gate))
    slope_two = sig_gate * (1.0 - sig_gate) * (2.0 + gate_preactivation * (1.0 - 2.0 * sig_gate))
    hidden_state = act_gate * up_preactivation
    tangent_hidden = slope_one * tangent_gate * up_preactivation + act_gate * tangent_up
    hidden_gradient = backward_baseline + adapter_scale * gated_product(
        projected_cotangent.T, adapter_down_factor
    )
    tangent_hidden_gradient = adapter_scale * (
        gated_product(tangent_projected_cotangent.T, adapter_down_factor)
        + gated_product(projected_cotangent.T, direction_down_adapter)
    )
    gate_gradient = hidden_gradient * up_preactivation * slope_one
    up_gradient = hidden_gradient * act_gate
    tangent_gate_gradient = (
        tangent_hidden_gradient * up_preactivation * slope_one
        + hidden_gradient * tangent_up * slope_one
        + hidden_gradient * up_preactivation * slope_two * tangent_gate
    )
    tangent_up_gradient = (
        tangent_hidden_gradient * act_gate + hidden_gradient * slope_one * tangent_gate
    )
    blended_gate = adapter_scale * (
        gated_product(direction_gate_adapter, gate_gradient.T)
        + gated_product(adapter_gate_factor, tangent_gate_gradient.T)
    )
    blended_up = adapter_scale * (
        gated_product(direction_up_adapter, up_gradient.T)
        + gated_product(adapter_up_factor, tangent_up_gradient.T)
    )
    tangent_reduced_down = gated_product(adapter_down_factor, tangent_hidden.T) + gated_product(
        direction_down_adapter, hidden_state.T
    )
    blended_product = lax.psum(jnp.stack([blended_gate, blended_up, tangent_reduced_down]), "fsdp")
    local_tokens = tokens.astype(jnp.float32)
    local_cotangent = cotangent.astype(jnp.float32)
    part_model = jnp.stack(
        [
            gated_product(blended_product[0], local_tokens),
            gated_product(blended_product[1], local_tokens),
            adapter_scale * gated_product(blended_product[2], local_cotangent),
        ]
    )
    part_hidden = jnp.stack(
        [
            adapter_scale
            * (
                gated_product(tangent_projected_gate, gate_gradient)
                + gated_product(projected_gate, tangent_gate_gradient)
            ),
            adapter_scale
            * (
                gated_product(tangent_projected_up, up_gradient)
                + gated_product(projected_up, tangent_up_gradient)
            ),
            adapter_scale
            * (
                gated_product(tangent_projected_cotangent, hidden_state)
                + gated_product(projected_cotangent, tangent_hidden)
            ),
        ]
    )
    curvature_model, curvature_hidden = lax.psum((part_model, part_hidden), "grp")
    beta = beta_prev[0]
    along_local = jnp.sum(curvature_model * direction_model) + jnp.sum(
        curvature_hidden * direction_hidden
    )
    square_local = jnp.sum(direction_model * direction_model) + jnp.sum(
        direction_hidden * direction_hidden
    )
    along, square = lax.psum((along_local, square_local), "fsdp")
    alpha = along / square
    resid_model = curvature_model - alpha * direction_model - beta * previous_model
    resid_hidden = curvature_hidden - alpha * direction_hidden - beta * previous_hidden
    total = lax.psum(
        jnp.sum(resid_model * resid_model) + jnp.sum(resid_hidden * resid_hidden), "fsdp"
    )
    factor = lax.rsqrt(total / (R * (3 * D + 3 * FF)) + 1e-06)
    return (resid_model * factor, resid_hidden * factor, jnp.reshape(alpha, (1,)))


def solution(mesh):
    placed = (
        P(("jobs", "grp"), "fsdp"),
        P(("jobs", "grp"), "fsdp"),
        P("grp", "fsdp"),
        P("grp", "fsdp"),
        P("fsdp", "grp"),
        P("jobs", None, "fsdp"),
        P("jobs", None, "fsdp"),
        P("jobs", None, "fsdp"),
        P("jobs", None, "fsdp"),
        P("jobs", None, "fsdp"),
        P("jobs", None, "fsdp"),
        P("jobs"),
    )
    return jax.shard_map(
        body,
        mesh=mesh,
        in_specs=placed,
        out_specs=(P("jobs", None, "fsdp"), P("jobs", None, "fsdp"), P("jobs")),
        check_vma=False,
    )
```

profile of v0, /device:TPU:0, one launch (start us, length us, event | category | flops | bytes accessed | tf_op | source)
XLA Modules:
  0.0 503.8 jit_solution(4711059674053161098)
XLA Ops:
  10.9 35.6 %all_gather.24 = bf16[3,16,8192]{2,1,0:T(8,128)(2,1)S(1)} all-gather(bf16[3,16,1024]{2,1,0:T(8,128)(2,1)S(1)} %convert_element_type.4), channel_id=1, replica_groups=mesh['jobs'=2,'fsdp'=8,'grp'=2] {'fsdp'}, dimensions={2}, use_global_device_ids=true | all-gather | bytes 884736 | tf_op jit(solution)/shard_map/all_gather | solution.py:49
  46.5 0.8 copy-done.6
  47.4 34.1 %all_gather.23 = bf16[3,16,8192]{2,1,0:T(8,128)(2,1)S(1)} all-gather(bf16[3,16,1024]{2,1,0:T(8,128)(2,1)S(1)} %copy-done.30), channel_id=1, replica_groups=mesh['jobs'=2,'fsdp'=8,'grp'=2] {'fsdp'}, dimensions={2}, use_global_device_ids=true | all-gather | bytes 884736 | tf_op jit(solution)/shard_map/all_gather | solution.py:48
  81.5 0.9 copy-done.7
  82.4 19.6 %all-gather.10.cloned.1.call-done = bf16[256,8192]{1,0:T(8,128)(2,1)} async-done(((bf16[256,1024]{1,0:T(8,128)(2,1)}), bf16[256,8192]{1,0:T(8,128)(2,1)}) %all-gather.10.cloned.1.call-update) | async-done | bytes 4194320 | tf_op jit(solution)/shard_map/all_gather | solution.py:52
  102.0 3.6 fusion
  105.6 1.0 fusion.53
  106.6 2.4 fusion.49
  109.0 67.9 %all-gather.6.cloned.1.call-done = bf16[256,8192]{1,0:T(8,128)(2,1)} async-done(((bf16[256,1024]{1,0:T(8,128)(2,1)}), bf16[256,8192]{1,0:T(8,128)(2,1)}) %all-gather.6.cloned.1.call-update) | async-done | bytes 4194320 | tf_op jit(solution)/shard_map/all_gather | solution.py:53
  176.9 3.5 fusion.2
  180.4 1.0 fusion.58
  181.5 2.4 fusion.5
  183.9 2.7 fusion.6
  186.6 41.4 %all-gather.14.cloned.1.call-done = bf16[8192,2048]{1,0:T(8,128)(2,1)} async-done(((bf16[4096,2048]{1,0:T(8,128)(2,1)}), bf16[8192,2048]{1,0:T(8,128)(2,1)}) %all-gather.14.cloned.1.call-update) | async-done | bytes 33554448 | tf_op jit(solution)/shard_map/all_gather | solution.py:43
  228.0 20.0 %fusion.80 = f32[256,2048]{1,0:T(8,128)S(1)} fusion(bf16[256,8192]{1,0:T(8,128)(2,1)} %all-gather.10.cloned.1.call-done, bf16[8192,2048]{1,0:T(8,128)(2,1)} %all-gather.14.cloned.1.call-done), kind=kOutput, calls=%fused_computation.119 | convolution fusion | flops 8589934592 | bytes 39845888 | tf_op jit(solution)/shard_map/dot_general | solution.py:55
  248.0 1.2 fusion.7
  249.2 32.7 %all-gather.8.cloned.1.call-done = bf16[2048,8192]{1,0:T(8,128)(2,1)} async-done(((bf16[2048,4096]{1,0:T(8,128)(2,1)}), bf16[2048,8192]{1,0:T(8,128)(2,1)}) %all-gather.8.cloned.1.call-update) | async-done | bytes 33554448 | tf_op jit(solution)/shard_map/all_gather | solution.py:46
  281.8 20.7 %fusion.78 = f32[256,2048]{1,0:T(8,128)} fusion(bf16[256,8192]{1,0:T(8,128)(2,1)} %all-gather.6.cloned.1.call-done, bf16[2048,8192]{1,0:T(8,128)(2,1)} %all-gather.8.cloned.1.call-done), kind=kOutput, calls=%fused_computation.117 | convolution fusion | flops 8589934592 | bytes 39845888 | tf_op jit(solution)/shard_map/dot_general | solution.py:57
  302.5 4.8 fusion.9
  307.4 28.3 %all-gather.12.cloned.1.call-done = bf16[8192,2048]{1,0:T(8,128)(2,1)} async-done(((bf16[4096,2048]{1,0:T(8,128)(2,1)}), bf16[8192,2048]{1,0:T(8,128)(2,1)}) %all-gather.12.cloned.1.call-update) | async-done | bytes 33554448 | tf_op jit(solution)/shard_map/all_gather | solution.py:44
  335.7 16.6 %fusion.79 = f32[256,2048]{1,0:T(8,128)S(1)} fusion(bf16[256,8192]{1,0:T(8,128)(2,1)} %all-gather.10.cloned.1.call-done, bf16[8192,2048]{1,0:T(8,128)(2,1)} %all-gather.12.cloned.1.call-done), kind=kOutput, calls=%fused_computation.118 | convolution fusion | flops 8589934592 | bytes 39845888 | tf_op jit(solution)/shard_map/dot_general | solution.py:56
  352.3 1.2 fusion.8
  353.9 1.5 fusion.37
  355.4 1.7 fusion.41
  358.3 4.7 fusion.21
  363.0 1.0 fusion.56
  364.0 2.0 copy-done.9
  366.1 1.5 fusion.24
  367.7 1.1 fusion.26
  368.7 1.1 fusion.28
  370.4 39.2 %psum.42 = f32[3,16,256]{2,1,0:T(8,128)} all-reduce(f32[3,16,256]{2,1,0:T(8,128)} %pad_maximum_fusion.2), channel_id=1, replica_groups=mesh['jobs'=2,'fsdp'=8,'grp'=2] {'fsdp'}, use_global_device_ids=true, to_apply=%region_0.0 | all-reduce | flops 12288 | bytes 98304 | tf_op jit(solution)/shard_map/psum | solution.py:128
  409.6 1.0 fusion.23
  410.7 1.0 convolution_bitcast_fusion
  411.7 1.0 convolution_bitcast_fusion.1
  412.8 4.0 fusion.32
  416.8 1.6 fusion.35
  418.4 1.8 fusion.39
  420.2 1.1 fusion.15
  421.8 1.1 fusion.13
  422.9 1.1 fusion.11
  425.5 16.3 %all-reduce.4.cloned.1.call-done = (f32[3,16,1024]{2,1,0:T(8,128)}, f32[3,16,2048]{2,1,0:T(8,128)}) async-done(((f32[3,16,1024]{2,1,0:T(8,128)}, f32[3,16,2048]{2,1,0:T(8,128)}), (f32[3,16,1024]{2,1,0:T(8,128)}, f32[3,16,2048]{2,1,0:T(8,128)})) %all-reduce.4.cloned.1.call-update) | async-done | bytes 589840 | tf_op jit(solution)/shard_map/psum | solution.py:157
  441.8 1.6 multiply_reduce_fusion.4
  443.5 1.7 multiply_reduce_fusion.1
  448.3 22.1 %all-reduce = (f32[]{:T(128)}, f32[]{:T(128)}) all-reduce(f32[]{:T(128)S(6)} %add.106, f32[]{:T(128)S(6)} %add.107), channel_id=1, replica_groups=mesh['jobs'=2,'fsdp'=8,'grp'=2] {'fsdp'}, use_global_device_ids=true, to_apply=%region_5.0 | all-reduce | flops 2 | bytes 16 | tf_op jit(solution)/shard_map/psum | solution.py:165
  471.8 1.6 multiply_reduce_fusion.3
  473.4 0.8 multiply_reduce_fusion
  475.5 17.6 %psum.47 = f32[]{:T(128)} all-reduce(f32[]{:T(128)S(6)} %add.108), channel_id=1, replica_groups=mesh['jobs'=2,'fsdp'=8,'grp'=2] {'fsdp'}, use_global_device_ids=true, to_apply=%region_11.0 | all-reduce | flops 1 | bytes 8 | tf_op jit(solution)/shard_map/psum | solution.py:169
  494.6 0.8 broadcast_multiply_fusion
  (83 shorter events, 8.7 us)
Async XLA Ops:
  7.2 94.8 %all-gather.10.cloned.1.call-start = ((), (), s32[]{:S(2)}) async-start(), calls=%async_computation.2 | async-start | bytes 4718592 | tf_op jit(solution)/shard_map/all_gather | solution.py:52
  7.9 169.0 %all-gather.6.cloned.1.call-start = ((), (), s32[]{:S(2)}) async-start(), calls=%async_computation | async-start | bytes 4718592 | tf_op jit(solution)/shard_map/all_gather | solution.py:53
  8.6 219.3 %all-gather.14.cloned.1.call-start = ((), (), s32[]{:S(2)}) async-start(), calls=%async_computation.4 | async-start | bytes 50331648 | tf_op jit(solution)/shard_map/all_gather | solution.py:43
  9.4 272.5 %all-gather.8.cloned.1.call-start = ((), (), s32[]{:S(2)}) async-start(), calls=%async_computation.1 | async-start | bytes 50331648 | tf_op jit(solution)/shard_map/all_gather | solution.py:46
  10.0 0.9 copy-start.21
  10.0 325.7 %all-gather.12.cloned.1.call-start = ((), (), s32[]{:S(2)}) async-start(), calls=%async_computation.3 | async-start | bytes 50331648 | tf_op jit(solution)/shard_map/all_gather | solution.py:44
  10.6 36.8 %copy-start.30 = (bf16[3,16,1024]{2,1,0:T(8,128)(2,1)S(1)}, bf16[3,16,1024]{2,1,0:T(8,128)(2,1)}, u32[]{:S(2)}) copy-start(bf16[3,16,1024]{2,1,0:T(8,128)(2,1)} %param.17) | copy-start | bytes 294916
  10.6 431.3 %all-reduce.4.cloned.1.call-start = ((), (), s32[]{:S(2)}) async-start(), calls=%async_computation.5 | async-start | bytes 1179648 | tf_op jit(solution)/shard_map/psum | solution.py:157
  46.5 0.9 copy-start.6
  46.5 35.9 %copy-start.5 = (f32[3,16,2048]{2,1,0:T(8,128)S(1)}, f32[3,16,2048]{2,1,0:T(8,128)}, u32[]{:S(2)}) copy-start(f32[3,16,2048]{2,1,0:T(8,128)} %param.20) | copy-start | bytes 1179652
  81.4 0.9 copy-start.7
  82.4 23.2 %copy-start.19 = (bf16[3,16,2048]{2,1,0:T(8,128)(2,1)S(1)}, bf16[3,16,2048]{2,1,0:T(8,128)(2,1)}, u32[]{:S(2)}) copy-start(bf16[3,16,2048]{2,1,0:T(8,128)(2,1)} %param.18) | copy-start | bytes 589828
  105.6 251.6 %copy-start.24 = (f32[4,16,256]{2,1,0:T(8,128)}, f32[4,16,256]{2,1,0:T(8,128)S(1)}, u32[]{:S(2)}) copy-start(f32[4,16,256]{2,1,0:T(8,128)S(1)} %fusion) | copy-start | bytes 196612
  105.6 71.3 %slice-start = ((bf16[3,16,8192]{2,1,0:T(8,128)(2,1)}), bf16[1,16,8192]{2,1,0:T(8,128)(2,1)S(1)}, s32[]{:S(2)}) async-start(bf16[3,16,8192]{2,1,0:T(8,128)(2,1)} %copy-done.6), calls=%async_computation.6 | async-start | bytes 524288 | tf_op jit(solution)/shard_map/slice | solution.py:20
  105.6 71.3 %slice-start.1 = ((bf16[3,16,8192]{2,1,0:T(8,128)(2,1)}), bf16[1,16,8192]{2,1,0:T(8,128)(2,1)S(1)}, s32[]{:S(2)}) async-start(bf16[3,16,8192]{2,1,0:T(8,128)(2,1)} %copy-done.7), calls=%async_computation.7 | async-start | bytes 524288 | tf_op jit(solution)/shard_map/slice | solution.py:20
  180.4 122.1 %copy-start.27 = (f32[2,16,256]{2,1,0:T(8,128)}, f32[2,16,256]{2,1,0:T(8,128)S(1)}, u32[]{:S(2)}) copy-start(f32[2,16,256]{2,1,0:T(8,128)S(1)} %fusion.2) | copy-start | bytes 98308
  249.1 106.2 %copy-start.8 = (f32[256,2048]{1,0:T(8,128)}, f32[256,2048]{1,0:T(8,128)S(1)}, u32[]{:S(2)}) copy-start(f32[256,2048]{1,0:T(8,128)S(1)} %fusion.7) | copy-start | bytes 6291460
  352.3 1.6 copy-start.11
  353.9 10.2 %copy-start.14 = (f32[256,2048]{1,0:T(8,128)}, f32[256,2048]{1,0:T(8,128)S(1)}, u32[]{:S(2)}) copy-start(f32[256,2048]{1,0:T(8,128)S(1)} %fusion.8) | copy-start | bytes 6291460
  355.4 1.8 copy-start.13
  355.4 2.2 copy-start.16
  355.4 2.8 copy-start.17
  362.9 4.7 copy-start.2
  362.9 4.7 copy-start
  363.0 3.1 copy-start.9
  366.1 1.6 copy-start.20
  367.6 42.0 %copy-start.18 = (bf16[256,1024]{1,0:T(8,128)(2,1)S(1)}, bf16[256,1024]{1,0:T(8,128)(2,1)}, u32[]{:S(2)}) copy-start(bf16[256,1024]{1,0:T(8,128)(2,1)} %param.13) | copy-start | bytes 1572868
  367.6 43.0 %copy-start.4 = (bf16[256,1024]{1,0:T(8,128)(2,1)S(1)}, bf16[256,1024]{1,0:T(8,128)(2,1)}, u32[]{:S(2)}) copy-start(bf16[256,1024]{1,0:T(8,128)(2,1)} %param.12) | copy-start | bytes 1572868
  412.7 4.0 copy-start.10
  412.7 4.0 copy-start.12
  412.7 4.0 copy-start.25
  416.8 1.6 copy-start.15
  418.4 1.8 copy-start.3
  418.4 1.8 copy-start.28
  420.2 1.6 copy-start.1
  422.9 18.9 %copy-start.22 = (f32[3,16,1024]{2,1,0:T(8,128)S(1)}, f32[3,16,1024]{2,1,0:T(8,128)}, u32[]{:S(2)}) copy-start(f32[3,16,1024]{2,1,0:T(8,128)} %param.19) | copy-start | bytes 589828
  422.9 48.9 %copy-start.29 = (f32[3,16,1024]{2,1,0:T(8,128)S(1)}, f32[3,16,1024]{2,1,0:T(8,128)}, u32[]{:S(2)}) copy-start(f32[3,16,1024]{2,1,0:T(8,128)} %param.21) | copy-start | bytes 589828
  424.0 49.4 %copy-start.26 = (f32[3,16,2048]{2,1,0:T(8,128)S(1)}, f32[3,16,2048]{2,1,0:T(8,128)}, u32[]{:S(2)}) copy-start(f32[3,16,2048]{2,1,0:T(8,128)} %param.22) | copy-start | bytes 1179652
  441.8 31.6 %copy-start.23 = (f32[3,16,2048]{2,1,0:T(8,128)S(1)}, f32[3,16,2048]{2,1,0:T(8,128)}, u32[]{:S(2)}) copy-start(f32[3,16,2048]{2,1,0:T(8,128)} %get-tuple-element.10) | copy-start | bytes 1179652
Sparse Core Ops, SparseCore 0:
  10.2 91.7 all-gather.9
  104.2 72.6 all-gather.5
  178.5 49.4 all-gather.13
  229.4 52.3 all-gather.7
  283.2 52.3 all-gather.11
  425.7 16.1 all-reduce.3
where the time goes:
time: 510 us; the launch traced here: 504 us
  waiting for transfers between devices  209 us (41%)
  blocking collectives  149 us (29%)
  matrix products  107 us (21%)
  between operations  22.6 us (4%)
  other arithmetic  9.31 us (2%)
  local copies, waits for them, and re-layouts  6.2 us (1%)
    all_gather x1, waiting for transfers between devices, body(): lax.all_gather(cotangent, 'fsdp', axis=1, tiled=True)  67.9 us
    dot_general x24, matrix products, gated_product(): jnp.dot(left, right, precision=lax.Precision.HIGHEST, preferred_element_t...  43.1 us
    all_gather x1, waiting for transfers between devices, body(): lax.all_gather(w_gate, 'grp', axis=0, tiled=True)  41.4 us
    psum x1, blocking collectives, body(): lax.psum(jnp.stack([blended_gate, blended_up, tangent_reduced_down]), 'fs...  39.2 us
    all_gather x1, blocking collectives, body(): lax.all_gather(dir_model, 'fsdp', axis=2, tiled=True)  35.6 us
    all_gather x1, blocking collectives, body(): lax.all_gather(adapt_model, 'fsdp', axis=2, tiled=True)  34.1 us
    all_gather x1, waiting for transfers between devices, body(): full_down = lax.all_gather(w_down, 'grp', axis=1, tiled=True)  32.7 us
    all_gather x1, waiting for transfers between devices, body(): lax.all_gather(w_up, 'grp', axis=0, tiled=True)  28.3 us
  transfers between devices with their start and end apart: 6, of which 6 were waited for; matrix products, arithmetic and copies ran while one was open for 13% of the time, Pallas kernels for 0%

commit v1 on v0

--- a/solution.py
+++ b/solution.py
@@ -1,6 +1,9 @@
+import functools
 import jax
 import jax.numpy as jnp
 from jax import lax
+from jax.experimental import pallas as pl
+from jax.experimental.pallas import tpu as pltpu
 from jax.sharding import PartitionSpec as P
 
 D = 8192
@@ -173,6 +176,551 @@
     return (resid_model * factor, resid_hidden * factor, jnp.reshape(alpha, (1,)))
 
 
+MESH = pl.DeviceIdType.MESH
+NT = (((1,), (1,)), ((), ()))
+NN = (((1,), (0,)), ((), ()))
+CHIPS = 8
+BLOCKS = 4
+GROUPS = 6
+TILE = 256
+
+
+def mm(left, right, dims=NN):
+    return lax.dot_general(left, right, dims, preferred_element_type=jnp.float32)
+
+
+def high_low(value):
+    high = value.astype(jnp.bfloat16)
+    return high, (value - high.astype(jnp.float32)).astype(jnp.bfloat16)
+
+
+def fused_kernel(
+    tok,
+    cot,
+    w_gate,
+    w_up,
+    w_down,
+    ad_m,
+    ad_h,
+    dir_m,
+    dir_h,
+    prev_m,
+    prev_h,
+    beta_ref,
+    out_m,
+    out_h,
+    out_a,
+    buf,
+    acc,
+    rbuf,
+    wgu,
+    wdn,
+    pp,
+    rsp,
+    pall,
+    prows,
+    left,
+    right,
+    hid,
+    mp,
+    rsm,
+    mall,
+    st,
+    h_m,
+    h_h,
+    own_sem,
+    w_sem,
+    sib_s,
+    z_s,
+    x_s,
+    c_r,
+    pr_s,
+    pr_r,
+    pg_s,
+    pg_r,
+    part_s,
+    part_r,
+    hid_s,
+    hid_r,
+    mr_s,
+    mr_r,
+    mg_s,
+    mg_r,
+    st_s,
+    st_r,
+):
+    job = lax.axis_index("jobs")
+    f = lax.axis_index("fsdp")
+    g = lax.axis_index("grp")
+    z = f // 2
+    x = lax.rem(f, 2)
+    o = 1 - g
+    rows = buf.shape[2]
+    depth = buf.shape[3]
+    cols = acc.shape[3]
+    home = (z // 2) == g
+    away = jnp.logical_not(home)
+    own = jnp.where(home, f - g * BLOCKS, BLOCKS)
+    sib_own = jnp.where(home, BLOCKS, f - o * BLOCKS)
+    near = jnp.where(home, z - 2 * g, 1 - g)
+    far = 1 - near
+    drains = []
+
+    def send(src, dst, ss, rs, dev, pred=None):
+        def make():
+            return pltpu.make_async_remote_copy(
+                src_ref=src, dst_ref=dst, send_sem=ss, recv_sem=rs, device_id=dev, device_id_type=MESH
+            )
+
+        if pred is None:
+            make().start()
+        else:
+            pl.when(pred)(lambda: make().start())
+        return make
+
+    def drain(make, pred=None):
+        drains.append((make, pred))
+
+    def landed(ref, rs):
+        pltpu.make_async_remote_copy(
+            src_ref=ref, dst_ref=ref, send_sem=sib_s.at[0], recv_sem=rs, device_id=(job, f, o), device_id_type=MESH
+        ).wait_recv()
+
+    for a, src in enumerate((tok, cot)):
+        pltpu.make_async_copy(src, buf.at[own, 2 * a + g], own_sem.at[a]).start()
+
+    order = [near * 2 + x, near * 2 + 1 - x, far * 2 + x, far * 2 + 1 - x]
+
+    def w_copy(piece):
+        stage, kind = piece // 3, piece % 3
+        at = pl.ds(pl.multiple_of(order[stage] * depth, depth), depth)
+        if kind < 2:
+            q = (2 * stage + kind) % 3
+            return pltpu.make_async_copy((w_gate, w_up)[kind].at[at, :], wgu.at[q], w_sem.at[q])
+        q = stage % 2
+        return pltpu.make_async_copy(w_down.at[:, at], wdn.at[q], w_sem.at[3 + q])
+
+    for piece in (0, 1, 2, 3, 5):
+        w_copy(piece).start()
+
+    barrier = pltpu.get_barrier_semaphore()
+    for r in range(CHIPS):
+        for t in range(2):
+
+            @pl.when(jnp.logical_or(f != r, g != t))
+            def _():
+                pl.semaphore_signal(barrier, inc=1, device_id=(job, r, t), device_id_type=MESH)
+
+    pl.semaphore_wait(barrier, 2 * CHIPS - 1)
+
+    for a, src in enumerate((tok, cot)):
+        drain(send(src, buf.at[sib_own, 2 * a + g], sib_s.at[a], c_r.at[sib_own, 2 * a + g], (job, f, o)))
+    for a, src in enumerate((tok, cot)):
+        pltpu.make_async_copy(src, buf.at[own, 2 * a + g], own_sem.at[a]).wait()
+
+    def relay(i, k, c):
+        zb = 2 * g + i
+        slot = i * 2 + x
+        ref = buf.at[slot, c]
+        sem = c_r.at[slot, c]
+        up = jnp.logical_and(z >= zb, z < 3)
+        down = jnp.logical_and(z <= zb, z > 0)
+        send(ref, ref, x_s.at[k, c], sem, (job, f + 1 - 2 * x, g))
+        send(ref, ref, z_s.at[0, k, c], sem, (job, f + 2, g), up)
+        send(ref, ref, z_s.at[1, k, c], sem, (job, f - 2, g), down)
+
+    def relay_drain(i, k, c):
+        zb = 2 * g + i
+        slot = i * 2 + x
+        ref = buf.at[slot, c]
+        sem = c_r.at[slot, c]
+        up = jnp.logical_and(z >= zb, z < 3)
+        down = jnp.logical_and(z <= zb, z > 0)
+
+        def make(ss, dev):
+            return pltpu.make_async_remote_copy(
+                src_ref=ref, dst_ref=ref, send_sem=ss, recv_sem=sem, device_id=dev, device_id_type=MESH
+            )
+
+        make(x_s.at[k, c], (job, f + 1 - 2 * x, g)).wait_send()
+
+        @pl.when(up)
+        def _():
+            make(z_s.at[0, k, c], (job, f + 2, g)).wait_send()
+
+        @pl.when(down)
+        def _():
+            make(z_s.at[1, k, c], (job, f - 2, g)).wait_send()
+
+    @pl.when(home)
+    def _():
+        for a in range(2):
+            relay(near, 0, 2 * a + g)
+        for a in range(2):
+            landed(buf.at[own, 2 * a + o], c_r.at[own, 2 * a + o])
+            relay(near, 0, 2 * a + o)
+
+    dir_b = dir_m[...].astype(jnp.bfloat16)
+    low_t = jnp.concatenate([ad_m[:2], dir_b[:2]], 0).reshape(64, depth)
+    low_c = jnp.concatenate([ad_m[2], dir_b[2]], 0)
+    got_t = mm(low_t, buf[own, g], NT)
+    got_c = mm(low_c, buf[own, 2 + g], NT)
+    for k, v in enumerate(
+        (got_t[0:16], got_t[16:32], got_c[0:16], got_t[32:48], got_t[48:64], got_c[16:32])
+    ):
+        pp[k] = v
+    for r in range(GROUPS):
+        other = f != r
+        drain(send(pp.at[r], rsp.at[f], pr_s.at[r], pr_r.at[f], (job, r, g), other), other)
+
+        @pl.when(f == r)
+        def _():
+            rsp[r] = pp[r]
+
+    @pl.when(away)
+    def _():
+        for c in range(4):
+            landed(buf.at[near * 2 + x, c], c_r.at[near * 2 + x, c])
+            relay(near, 0, c)
+
+    def product(kind, stage, half, first):
+        q = (2 * stage + kind) % 3 if kind < 2 else stage % 2
+        a = 0 if kind < 2 else 1
+        slot = order[stage]
+
+        def step(n, carry):
+            at = pl.ds(pl.multiple_of(n * TILE, TILE), TILE)
+            wat = pl.ds(pl.multiple_of(half * cols + n * TILE, TILE), TILE)
+            value = buf[slot, 2 * a : 2 * a + 2].reshape(2 * rows, depth)
+            if kind < 2:
+                got = mm(value, wgu[q, :, wat])
+            else:
+                got = mm(value, wdn[q, wat, :], NT)
+            if not first:
+                got = acc[kind, half, :, at] + got
+            acc[kind, half, :, at] = got
+            return carry
+
+        lax.fori_loop(0, cols // TILE, step, 0)
+
+    def after(piece):
+        kind, stage = piece % 3, piece // 3
+        if kind < 2:
+            nxt = 2 * stage + kind + 3
+            if nxt < 8:
+                w_copy((nxt // 2) * 3 + nxt % 2).start()
+        elif stage + 2 < 4:
+            w_copy((stage + 2) * 3 + 2).start()
+
+    def compute(stage):
+        for kind in range(3):
+            w_copy(stage * 3 + kind).wait()
+            for half in range(2):
+                product(kind, stage, half, stage == 0)
+            after(stage * 3 + kind)
+
+    compute(0)
+    for c in range(4):
+        landed(buf.at[far * 2 + x, c], c_r.at[far * 2 + x, c])
+        relay(far, 1, c)
+
+    @pl.when(f < GROUPS)
+    def _():
+        for s in range(CHIPS):
+
+            @pl.when(f != s)
+            def _():
+                landed(rsp.at[s], pr_r.at[s])
+
+        pall[f, g] = jnp.sum(rsp[...], axis=0)
+
+    for r in range(CHIPS):
+        for t in range(2):
+            pred = jnp.logical_and(f < GROUPS, jnp.logical_or(f != r, g != t))
+            drain(
+                send(pall.at[f, g], pall.at[f, g], pg_s.at[2 * r + t], pg_r.at[f, g], (job, r, t), pred), pred
+            )
+
+    for c in range(4):
+        landed(buf.at[near * 2 + 1 - x, c], c_r.at[near * 2 + 1 - x, c])
+    compute(1)
+    compute(2)
+
+    for r in range(GROUPS):
+        for t in range(2):
+
+            @pl.when(jnp.logical_or(f != r, g != t))
+            def _():
+                landed(pall.at[r, t], pg_r.at[r, t])
+
+    for r in range(8):
+        for t in range(2):
+            at = slice(t * rows, (t + 1) * rows)
+            if r < GROUPS:
+                prows[16 * r : 16 * r + 16, at] = pall[r, t]
+            else:
+                prows[16 * r : 16 * r + 16, at] = jnp.zeros((16, rows), jnp.float32)
+    turned = jnp.transpose(prows[...])
+    t_high, t_low = high_low(turned)
+    left[:, 0:128] = t_high
+    left[:, 128:256] = t_low
+    mine = pl.ds(pl.multiple_of(g * cols, cols), cols)
+    right[...] = jnp.zeros(right.shape, right.dtype)
+    for k in range(3):
+        b = ad_h[k, :, mine] * jnp.bfloat16(2.0)
+        v = dir_h[k, :, mine].astype(jnp.bfloat16) * jnp.bfloat16(2.0)
+        for base in (0, 128):
+            right[k, base + 16 * k : base + 16 * k + 16, :] = b
+            right[3 + k, base + 48 + 16 * k : base + 64 + 16 * k, :] = b
+            right[3 + k, base + 16 * k : base + 16 * k + 16, :] = v
+    hid[g] = jnp.zeros(hid.shape[1:], jnp.float32)
+    mp[...] = jnp.zeros(mp.shape, jnp.float32)
+    p_high, p_low = high_low(prows[...])
+
+    for c in range(4):
+        landed(buf.at[far * 2 + 1 - x, c], c_r.at[far * 2 + 1 - x, c])
+    for kind in range(3):
+        w_copy(9 + kind).wait()
+        product(kind, 3, o, False)
+        drain(send(acc.at[kind, o], rbuf.at[kind], part_s.at[kind], part_r.at[kind], (job, f, o)))
+    for kind in range(3):
+        product(kind, 3, g, False)
+    for kind in range(3):
+        landed(rbuf.at[kind], part_r.at[kind])
+
+    for t in range(2):
+        rat = slice(t * rows, (t + 1) * rows)
+        lft = left[rat, :]
+        ph = p_high[:, rat]
+        pw = p_low[:, rat]
+        pairs = [
+            (
+                jnp.concatenate([ph[16 * k : 16 * k + 16], pw[16 * k : 16 * k + 16]], 0),
+                jnp.concatenate([ph[48 + 16 * k : 64 + 16 * k], pw[48 + 16 * k : 64 + 16 * k]], 0),
+            )
+            for k in range(3)
+        ]
+
+        def step(n, carry, t=t, rat=rat, lft=lft, pairs=pairs):
+            at = pl.ds(pl.multiple_of(n * TILE, TILE), TILE)
+            hat = pl.ds(pl.multiple_of(g * cols + n * TILE, TILE), TILE)
+
+            def base(k):
+                return acc[k, g, rat, at] + rbuf[k, rat, at] + mm(lft, right[k, :, at])
+
+            gate = base(0)
+            up = base(1)
+            grad = base(2)
+            tan_gate = mm(lft, right[3, :, at])
+            tan_up = mm(lft, right[4, :, at])
+            tan_grad = mm(lft, right[5, :, at])
+            sg = jax.nn.sigmoid(gate)
+            act = gate * sg
+            rest = 1.0 - sg
+            one = sg * (1.0 + gate * rest)
+            two = sg * rest * (2.0 + gate * (1.0 - 2.0 * sg))
+            up_one = up * one
+            one_tan = one * tan_gate
+            values = (
+                (grad * up_one, tan_grad * up_one + grad * (tan_up * one + up * (two * tan_gate))),
+                (grad * act, tan_grad * act + grad * one_tan),
+                (act * up, one_tan * up + act * tan_up),
+            )
+            for k in range(3):
+                first, first_low = high_low(values[k][0])
+                second, second_low = high_low(values[k][1])
+                b = ad_h[k, :, hat]
+                v = dir_h[k, :, hat].astype(jnp.bfloat16)
+                part = (mm(v, first, NT) + mm(b, second, NT)) + (mm(v, first_low, NT) + mm(b, second_low, NT))
+                mp[2 * k, t] += part[0:8]
+                mp[2 * k + 1, t] += part[8:16]
+                q = mm(pairs[k][1], first) + mm(pairs[k][0], second)
+                w = mm(pairs[k][1][0:16], first_low) + mm(pairs[k][0][0:16], second_low)
+                hid[g, k, :, at] += 2.0 * (q[0:16] + (q[16:32] + w))
+            return carry
+
+        lax.fori_loop(0, cols // TILE, step, 0)
+
+    for r in range(GROUPS):
+        for t in range(2):
+            other = jnp.logical_or(f != r, g != t)
+            drain(
+                send(mp.at[r, t], rsm.at[f, g], mr_s.at[r, t], mr_r.at[f, g], (job, r, t), other), other
+            )
+
+            @pl.when(jnp.logical_not(other))
+            def _():
+                rsm[r, t] = mp[r, t]
+
+    drain(send(hid.at[g], hid.at[g], hid_s.at[0], hid_r.at[0], (job, f, o)))
+
+    @pl.when(f < GROUPS)
+    def _():
+        for r in range(CHIPS):
+            for t in range(2):
+
+                @pl.when(jnp.logical_or(f != r, g != t))
+                def _():
+                    landed(rsm.at[r, t], mr_r.at[r, t])
+
+        mall[f, g] = jnp.sum(rsm[...].reshape(2 * CHIPS, 8, rows), axis=0)
+
+    for r in range(CHIPS):
+        for t in range(2):
+            pred = jnp.logical_and(f < GROUPS, jnp.logical_or(f != r, g != t))
+            drain(
+                send(mall.at[f, g], mall.at[f, g], mg_s.at[2 * r + t], mg_r.at[f, g], (job, r, t), pred), pred
+            )
+
+    @pl.when(away)
+    def _():
+        for a in range(2):
+            landed(buf.at[own, 2 * a + o], c_r.at[own, 2 * a + o])
+
+    landed(hid.at[o], hid_r.at[0])
+    beta = beta_ref[0]
+    dh = dir_h[...]
+    hh = jnp.concatenate([hid[0], hid[1]], axis=-1)
+    hh2 = hh - beta * prev_h[...]
+    dm = dir_m[...]
+
+    for r in range(GROUPS):
+        for t in range(2):
+
+            @pl.when(jnp.logical_or(f != r, g != t))
+            def _():
+                landed(mall.at[r, t], mg_r.at[r, t])
+
+    whole = jnp.concatenate(
+        [jnp.concatenate([mall[r, 0], mall[r, 1]], axis=-1) for r in range(GROUPS)], axis=0
+    )
+    m_high, m_low = high_low(whole)
+    own_t = buf[own, 0:2].reshape(2 * rows, depth)
+    own_c = buf[own, 2:4].reshape(2 * rows, depth)
+    res_t = mm(jnp.concatenate([m_high[0:32], m_low[0:32]], 0), own_t)
+    res_c = mm(jnp.concatenate([m_high[32:48], m_low[32:48]], 0), own_c)
+    hm = 2.0 * jnp.concatenate([res_t[0:32] + res_t[32:64], res_c[0:16] + res_c[16:32]], 0).reshape(
+        3, 16, depth
+    )
+    hm2 = hm - beta * prev_m[...]
+
+    def total(v, w):
+        return jnp.sum(v) + jnp.sum(w)
+
+    square = total(dm * dm, dh * dh)
+    along = total(hm * dm, hh * dh)
+    along2 = total(hm2 * dm, hh2 * dh)
+    slope = jnp.where(square > 0.0, along2 / jnp.where(square > 0.0, square, 1.0), 0.0)
+    em = hm2 - slope * dm
+    eh = hh2 - slope * dh
+    left_over = total(em * em, eh * eh)
+    h_m[...] = hm2
+    h_h[...] = hh2
+    line = lax.broadcasted_iota(jnp.int32, (8, 128), 0)
+    tile = jnp.where(
+        line == 0, square, jnp.where(line == 1, along, jnp.where(line == 2, slope, left_over))
+    )
+    st[f] = tile
+    for r in range(CHIPS):
+        other = f != r
+        drain(send(st.at[f], st.at[f], st_s.at[r], st_r.at[f], (job, r, g), other), other)
+    for r in range(CHIPS):
+
+        @pl.when(f != r)
+        def _():
+            landed(st.at[r], st_r.at[r])
+
+    every = st[...]
+    sq, al, sl, lo = (every[:, k, :] for k in range(4))
+    alpha = jnp.sum(al, axis=0, keepdims=True) / jnp.sum(sq, axis=0, keepdims=True)
+    away_sq = (alpha - sl) * (alpha - sl) * sq
+    ms = jnp.sum(lo + away_sq, axis=0, keepdims=True) / float(R * (3 * D + 3 * FF))
+    factor = lax.rsqrt(ms + 1e-06)
+    out_a[...] = alpha
+    one_alpha = alpha[0:1, 0:1].reshape(1, 1, 1)
+    one_factor = factor[0:1, 0:1].reshape(1, 1, 1)
+    out_m[...] = (h_m[...] - one_alpha * dir_m[...]) * one_factor
+    out_h[...] = (h_h[...] - one_alpha * dir_h[...]) * one_factor
+
+    for k, i in enumerate((near, far)):
+        for c in range(4):
+            relay_drain(i, k, c)
+    for make, pred in drains:
+        if pred is None:
+            make().wait_send()
+        else:
+            pl.when(pred)(lambda make=make: make().wait_send())
+
+
+def fused_body(tok, cot, w_gate, w_up, w_down, ad_m, ad_h, dir_m, dir_h, prev_m, prev_h, beta):
+    rows, depth = tok.shape
+    units = w_gate.shape[1]
+    cols = units // 2
+    bf, f32 = jnp.bfloat16, jnp.float32
+    vmem = pl.BlockSpec(memory_space=pltpu.VMEM)
+    hbm = pl.BlockSpec(memory_space=pl.ANY)
+    dma = pltpu.SemaphoreType.DMA
+    next_m, next_h, alpha = pl.pallas_call(
+        fused_kernel,
+        out_shape=(
+            jax.ShapeDtypeStruct(dir_m.shape, f32),
+            jax.ShapeDtypeStruct(dir_h.shape, f32),
+            jax.ShapeDtypeStruct((1, 128), f32),
+        ),
+        in_specs=[hbm] * 5 + [vmem] * 6 + [pl.BlockSpec(memory_space=pltpu.SMEM)],
+        out_specs=(vmem, vmem, vmem),
+        scratch_shapes=[
+            pltpu.VMEM((BLOCKS + 1, 4, rows, depth), bf),
+            pltpu.VMEM((3, 2, 2 * rows, cols), f32),
+            pltpu.VMEM((3, 2 * rows, cols), f32),
+            pltpu.VMEM((3, depth, units), bf),
+            pltpu.VMEM((2, units, depth), bf),
+            pltpu.VMEM((GROUPS, 16, rows), f32),
+            pltpu.VMEM((CHIPS, 16, rows), f32),
+            pltpu.VMEM((GROUPS, 2, 16, rows), f32),
+            pltpu.VMEM((128, 2 * rows), f32),
+            pltpu.VMEM((2 * rows, 256), bf),
+            pltpu.VMEM((6, 256, cols), bf),
+            pltpu.VMEM((2, 3, 16, cols), f32),
+            pltpu.VMEM((GROUPS, 2, 8, rows), f32),
+            pltpu.VMEM((CHIPS, 2, 8, rows), f32),
+            pltpu.VMEM((GROUPS, 2, 8, rows), f32),
+            pltpu.VMEM((CHIPS, 8, 128), f32),
+            pltpu.VMEM(dir_m.shape, f32),
+            pltpu.VMEM(dir_h.shape, f32),
+            dma((2,)),
+            dma((5,)),
+            dma((2,)),
+            dma((2, 2, 4)),
+            dma((2, 4)),
+            dma((BLOCKS + 1, 4)),
+            dma((GROUPS,)),
+            dma((CHIPS,)),
+            dma((2 * CHIPS,)),
+            dma((GROUPS, 2)),
+            dma((3,)),
+            dma((3,)),
+            dma((1,)),
+            dma((1,)),
+            dma((GROUPS, 2)),
+            dma((CHIPS, 2)),
+            dma((2 * CHIPS,)),
+            dma((GROUPS, 2)),
+            dma((CHIPS,)),
+            dma((CHIPS,)),
+        ],
+        compiler_params=pltpu.CompilerParams(
+            collective_id=0, has_side_effects=True, vmem_limit_bytes=62 * 1024 * 1024
+        ),
+        cost_estimate=pl.CostEstimate(
+            flops=6 * 2 * rows * BLOCKS * depth * units,
+            bytes_accessed=6 * BLOCKS * depth * units,
+            transcendentals=2 * rows * cols,
+        ),
+    )(tok, cot, w_gate, w_up, w_down, ad_m, ad_h, dir_m, dir_h, prev_m, prev_h, beta)
+    return next_m, next_h, alpha[0, :1]
+
+
 def solution(mesh):
     placed = (
         P(("jobs", "grp"), "fsdp"),
@@ -188,8 +736,10 @@
         P("jobs", None, "fsdp"),
         P("jobs"),
     )
+    chips = mesh.shape["fsdp"]
+    use = fused_body if chips == 8 and mesh.shape["grp"] == 2 else body
     return jax.shard_map(
-        body,
+        use,
         mesh=mesh,
         in_specs=placed,
         out_specs=(P("jobs", None, "fsdp"), P("jobs", None, "fsdp"), P("jobs")),

time: 510 us -> 153 us (0.30); the launches traced: 504 us -> 153 us
  waiting for transfers between devices: 209 us -> 0 us
  blocking collectives: 149 us -> 0 us
  Pallas kernels: 0 us -> 146 us
  matrix products: 107 us -> 0 us
  between operations: 22.6 us -> 3.09 us
  other arithmetic: 9.31 us -> 0 us
    all_gather x5 -> x0, waiting for transfers between devices: 190 us -> none  [the longest x1 67.9 us: body(): lax.all_gather(cotangent, 'fsdp', axis=1, tiled=True)]
    pallas_call x0 -> x1, Pallas kernels: none -> 146 us  [fused_body(): pl.pallas_call(fused_kernel, out_shape=(jax.ShapeDtypeStruct(dir_m.shape,...]
    dot_general x29 -> x0, matrix products: 107 us -> none  [the longest x24 43.1 us: gated_product(): jnp.dot(left, right, precision=lax.Precision.HIGHEST, preferred_element_t...]
    psum x3 -> x0, blocking collectives: 79 us -> none  [the longest x1 39.2 us: body(): lax.psum(jnp.stack([blended_gate, blended_up, tangent_reduced_down]), 'fs...]
    all_gather x2 -> x0, blocking collectives: 69.6 us -> none  [the longest x1 35.6 us: body(): lax.all_gather(dir_model, 'fsdp', axis=2, tiled=True)]
    psum x1 -> x0, waiting for transfers between devices: 16.3 us -> none  [body(): lax.psum((part_model, part_hidden), 'grp')]
    reduce_sum x4 -> x0, other arithmetic: 5.71 us -> none  [the longest x1 1.7 us: body(): jnp.sum(direction_hidden * direction_hidden)]
  transfers between devices with their start and end apart: 6 -> 0, of which waited for: 6 -> 0; matrix products, arithmetic and copies ran while one was open for 13% -> 0% of each run, Pallas kernels for 0% -> 0%
where the time goes in v1:
time: 153 us
  Pallas kernels  146 us (95%)
  local copies, waits for them, and re-layouts  3.38 us (2%)
  between operations  3.09 us (2%)
    pallas_call x1, Pallas kernels, fused_body(): pl.pallas_call(fused_kernel, out_shape=(jax.ShapeDtypeStruct(dir_m.shape,...  146 us
    unnamed x2, local copies, waits for them, and re-layouts  3.38 us

profile of v1, /device:TPU:0, one launch (start us, length us, event | category | flops | bytes accessed | tf_op | source)
XLA Modules:
  0.0 152.7 jit_solution(12251009689685999149)
XLA Ops:
  1.3 146.2 %shard_map.139 = (f32[3,16,1024]{2,1,0:T(8,128)}, f32[3,16,2048]{2,1,0:T(8,128)}, f32[1,128]{1,0:T(1,128)}) custom-call(bf16[256,1024]{1,0:T(8,128)(2,1)} %tok.1, bf16[256,1024]{1,0:T(8,128)(2,1)} %cot.1, bf16[4096,2048]{1,0:T(8,128)(2,1)} %w_gate.1, bf16[4096,2048]{1,0:T(8,128)(2,1)} %w_up.1, bf16[2048,4096]{1,0:T(8,128)(2,1)} %w_down.1, ...), custom_call_target="tpu_custom_call" | custom-call | flops 25769803776 | bytes 50331648 | tf_op jit(solution)/shard_map/pallas_call | solution.py:663
  147.5 1.6 %copy.19 = f32[3,16,1024]{2,1,0:T(8,128)} copy(f32[3,16,1024]{2,1,0:T(8,128)} %get-tuple-element.12) | data formatting | bytes 393216
  149.1 1.8 %copy.20 = f32[3,16,2048]{2,1,0:T(8,128)} copy(f32[3,16,2048]{2,1,0:T(8,128)} %get-tuple-element.13) | data formatting | bytes 786432

commit v2 on v1

--- a/solution.py
+++ b/solution.py
@@ -325,9 +325,9 @@
         sem = c_r.at[slot, c]
         up = jnp.logical_and(z >= zb, z < 3)
         down = jnp.logical_and(z <= zb, z > 0)
-        send(ref, ref, x_s.at[k, c], sem, (job, f + 1 - 2 * x, g))
         send(ref, ref, z_s.at[0, k, c], sem, (job, f + 2, g), up)
         send(ref, ref, z_s.at[1, k, c], sem, (job, f - 2, g), down)
+        send(ref, ref, x_s.at[k, c], sem, (job, f + 1 - 2 * x, g))
 
     def relay_drain(i, k, c):
         zb = 2 * g + i
@@ -477,14 +477,21 @@
     mp[...] = jnp.zeros(mp.shape, jnp.float32)
     p_high, p_low = high_low(prows[...])
 
-    for c in range(4):
-        landed(buf.at[far * 2 + 1 - x, c], c_r.at[far * 2 + 1 - x, c])
-    for kind in range(3):
+    def last(kind):
         w_copy(9 + kind).wait()
         product(kind, 3, o, False)
         drain(send(acc.at[kind, o], rbuf.at[kind], part_s.at[kind], part_r.at[kind], (job, f, o)))
-    for kind in range(3):
-        product(kind, 3, g, False)
+
+    for c in (0, 1):
+        landed(buf.at[far * 2 + 1 - x, c], c_r.at[far * 2 + 1 - x, c])
+    last(0)
+    last(1)
+    product(0, 3, g, False)
+    product(1, 3, g, False)
+    for c in (2, 3):
+        landed(buf.at[far * 2 + 1 - x, c], c_r.at[far * 2 + 1 - x, c])
+    last(2)
+    product(2, 3, g, False)
     for kind in range(3):
         landed(rbuf.at[kind], part_r.at[kind])
 

time: 153 us -> 154 us (level)
  no operation moved by 1% of the time
where the time goes in v2:
time: 154 us
  Pallas kernels  147 us (95%)
  local copies, waits for them, and re-layouts  3.38 us (2%)
  between operations  3.09 us (2%)
    pallas_call x1, Pallas kernels, fused_body(): pl.pallas_call(fused_kernel, out_shape=(jax.ShapeDtypeStruct(dir_m.shape,...  147 us
    unnamed x2, local copies, waits for them, and re-layouts  3.38 us

profile of v2, /device:TPU:0, one launch (start us, length us, event | category | flops | bytes accessed | tf_op | source)
XLA Modules:
  0.0 153.5 jit_solution(12640790136266801189)
XLA Ops:
  1.3 147.1 %shard_map.139 = (f32[3,16,1024]{2,1,0:T(8,128)}, f32[3,16,2048]{2,1,0:T(8,128)}, f32[1,128]{1,0:T(1,128)}) custom-call(bf16[256,1024]{1,0:T(8,128)(2,1)} %tok.1, bf16[256,1024]{1,0:T(8,128)(2,1)} %cot.1, bf16[4096,2048]{1,0:T(8,128)(2,1)} %w_gate.1, bf16[4096,2048]{1,0:T(8,128)(2,1)} %w_up.1, bf16[2048,4096]{1,0:T(8,128)(2,1)} %w_down.1, ...), custom_call_target="tpu_custom_call" | custom-call | flops 25769803776 | bytes 50331648 | tf_op jit(solution)/shard_map/pallas_call | solution.py:670
  148.4 1.6 %copy.19 = f32[3,16,1024]{2,1,0:T(8,128)} copy(f32[3,16,1024]{2,1,0:T(8,128)} %get-tuple-element.12) | data formatting | bytes 393216
  150.0 1.8 %copy.20 = f32[3,16,2048]{2,1,0:T(8,128)} copy(f32[3,16,2048]{2,1,0:T(8,128)} %get-tuple-element.13) | data formatting | bytes 786432
